TPU v7x, 1024 devices: a whole 4x8x16 slice. The times are simulated.
1024 devices in a mesh: dp: 128 (over z, x, core), node: 8 (over y).
Axes of the slice: x: 4, y: 8, z: 16, core: 2. Of those that a mesh axis runs over, the one named last changes fastest.
Arguments:
- tokens: bfloat16 [131072, 4096], P('dp', 'node'), may hold values from -24 to 24
- weight_codes: bfloat16 [4096, 1024], P(('node', 'dp')), may hold values from -127 to 127, as said below
- block_scales: bfloat16 [4096, 4], P(('node', 'dp')), may hold values from 4.9829483e-05 to 0.00049972534
- cotangent: bfloat16 [131072, 1024], P('dp', 'node'), may hold values from -6 to 6
Outputs:
- values: bfloat16 [131072, 1024], P('dp', 'node')
- token_grad: bfloat16 [131072, 4096], P('dp', 'node')
- weight_grad: float32 [4096, 1024], P(('node', 'dp'))
Inputs may be any that keep to these rules, and one draw needn't show every extreme that they name: `weight_codes`: every entry is a whole number.
All inputs are finite; a program needn't handle non-finite values.
Results may differ from a plain program's by a relative error of at most 0.017.
Values may be sent and summed in bfloat16 or wider, within the bound.
A program may use at most 32 MiB of HBM per device.

v0:
```python
import math

import jax
import jax.numpy as jnp
from jax import lax
from jax.sharding import PartitionSpec as P


def dequantize(code_rows, scales):
    blocks = scales.shape[1]
    grouped = code_rows.astype(jnp.float32).reshape(code_rows.shape[0], blocks, -1)
    scaled = grouped * scales.astype(jnp.float32)[:, :, None]
    return scaled.reshape(code_rows.shape).astype(jnp.bfloat16)


def on_device(tokens, weight_codes, block_scales, cotangent):
    tok_rows = tokens.shape[0]
    grad_scale = 1.0 / math.sqrt(tok_rows * lax.axis_size("dp"))
    code_all, scale_all = (
        lax.all_gather(weight_codes, "dp", axis=0, tiled=True),
        lax.all_gather(block_scales, "dp", axis=0, tiled=True),
    )
    weight = dequantize(code_all, scale_all)
    partial_value = jnp.dot(tokens, weight, preferred_element_type=jnp.float32)
    partial_value = partial_value.astype(jnp.bfloat16)
    values = (
        lax.psum_scatter(partial_value, "node", scatter_dimension=1, tiled=True)
        .astype(jnp.float32)
        .astype(jnp.bfloat16)
    )
    full_cot = lax.all_gather(cotangent, "node", axis=1, tiled=True)
    code_again, scale_again = (
        lax.all_gather(weight_codes, "dp", axis=0, tiled=True),
        lax.all_gather(block_scales, "dp", axis=0, tiled=True),
    )
    weight = dequantize(code_again, scale_again)
    token_grad = lax.dot_general(
        full_cot, weight, (((1,), (1,)), ((), ())), preferred_element_type=jnp.float32
    ).astype(jnp.bfloat16)
    term = lax.dot_general(
        tokens, full_cot, (((0,), (0,)), ((), ())), preferred_element_type=jnp.float32
    )
    term = term * jnp.float32(grad_scale)
    weight_grad = lax.psum_scatter(term, "dp", scatter_dimension=0, tiled=True)
    return (values, token_grad, weight_grad)


def solution(mesh):
    placed = (P("dp", "node"), P(("node", "dp"), None), P(("node", "dp"), None), P("dp", "node"))
    return jax.shard_map(
        on_device,
        mesh=mesh,
        in_specs=placed,
        out_specs=(P("dp", "node"), P("dp", "node"), P(("node", "dp"), None)),
        check_vma=False,
    )
```

profile of v0, /device:TPU:1, one launch (start us, length us, event | category | flops | bytes accessed | tf_op | source)
XLA Modules:
  0.0 630.2 jit_solution(17220364369625445377)
XLA Ops:
  7.2 0.0 copy-start
  7.2 0.0 all-gather.5.cloned.1.call-start
  7.2 0.7 all-gather.5.cloned.1.call-update
  7.9 0.0 all-gather.7.cloned.1.call-start
  8.0 0.7 all-gather.7.cloned.1.call-update
  8.7 0.0 all-reduce.3.cloned.1.call-start
  8.7 61.9 %all-gather.5.cloned.1.call-done = bf16[1024,1024]{1,0:T(8,128)(2,1)} async-done(((bf16[1024,128]{1,0:T(8,128)(2,1)}), bf16[1024,1024]{1,0:T(8,128)(2,1)}) %all-gather.5.cloned.1.call-update) | async-done | bytes 2097168 | tf_op jit(solution)/shard_map/all_gather | solution.py:31
  70.6 0.0 copy-done
  70.6 4.2 convolution_multiply_fusion
  74.8 0.0 copy-start.3
  74.8 0.0 all-reduce.3.cloned.1.call-update
  74.8 0.0 reduce-scatter.2.cloned.1.call-start
  74.8 0.6 copy-done.3
  75.4 89.5 %all-gather.1 = bf16[128,4,4]{2,1,0:T(4,128)(2,1)S(1)} all-gather(bf16[1,4,4]{2,1,0:T(4,128)(2,1)S(1)} %bitcast.21), channel_id=1, replica_groups=mesh['dp'=128,'node'=8] {'dp'}, dimensions={0}, use_global_device_ids=true | all-gather | bytes 4128 | tf_op jit(solution)/shard_map/all_gather | solution.py:21
  164.9 0.6 mul.21
  165.6 0.5 copy.11
  166.0 50.4 %all-gather.7.cloned.1.call-done = bf16[128,4,1024]{2,1,0:T(4,128)(2,1)} async-done(((bf16[1,4,1024]{2,1,0:T(4,128)(2,1)}), bf16[128,4,1024]{2,1,0:T(4,128)(2,1)}) %all-gather.7.cloned.1.call-update) | async-done | bytes 1048592 | tf_op jit(solution)/shard_map/all_gather | solution.py:20
  216.4 2.5 reshape.16
  218.9 1.9 multiply_convert_fusion
  220.8 0.0 copy-start.2
  220.8 1.0 copy-done.2
  221.7 2.6 convert_bitcast_fusion
  224.4 0.0 copy-start.1
  224.4 0.0 reduce-scatter.2.cloned.1.call-update
  224.4 1.4 dynamic-slice
  226.5 0.0 copy-done.1
  226.5 3.5 fusion
  230.0 2.3 copy.10
  232.3 343.3 %all-reduce.3.cloned.1.call-done = f32[512,1024]{1,0:T(8,128)} async-done(((f32[512,1024]{1,0:T(8,128)}), f32[512,1024]{1,0:T(8,128)}) %all-reduce.3.cloned.1.call-update) | async-done | bytes 2097168
  575.6 1.4 constant_dynamic-slice_fusion
  577.0 44.9 %reduce-scatter.2.cloned.1.call-done = bf16[1024,128]{0,1:T(8,128)(2,1)} async-done(((bf16[1024,1024]{0,1:T(8,128)(2,1)}), bf16[1024,128]{0,1:T(8,128)(2,1)}) %reduce-scatter.2.cloned.1.call-update) | async-done | bytes 262160 | tf_op jit(solution)/shard_map/reduce_scatter | solution.py:27
  621.9 1.8 copy.9
Async XLA Ops:
  7.2 63.4 %copy-start = (bf16[1024,512]{1,0:T(8,128)(2,1)S(1)}, bf16[1024,512]{1,0:T(8,128)(2,1)}, u32[]{:S(2)}) copy-start(bf16[1024,512]{1,0:T(8,128)(2,1)} %param.4) | copy-start | bytes 3145732
  7.2 63.4 %all-gather.5.cloned.1.call-start = ((), (), s32[]{:S(2)}) async-start(), calls=%async_computation.2 | async-start | bytes 2359296 | tf_op jit(solution)/shard_map/all_gather | solution.py:31
  7.9 208.5 %all-gather.7.cloned.1.call-start = ((), (), s32[]{:S(2)}) async-start(), calls=%async_computation.3 | async-start | bytes 1056768 | tf_op jit(solution)/shard_map/all_gather | solution.py:20
  8.7 566.9 %all-reduce.3.cloned.1.call-start = ((), (), s32[]{:S(2)}) async-start(), calls=%async_computation.4 | async-start | bytes 4194304
  74.8 0.7 copy-start.3
  74.8 547.1 %reduce-scatter.2.cloned.1.call-start = ((), (), s32[]{:S(2)}) async-start(), calls=%async_computation.1 | async-start | bytes 2359296 | tf_op jit(solution)/shard_map/reduce_scatter | solution.py:27
  220.8 1.0 copy-start.2
  224.4 2.1 copy-start.1
Sparse Core Ops, SparseCore 0:
  10.6 59.9 all-gather.4
  74.7 141.6 all-gather.6
  219.8 355.7 all-reduce.2
  579.3 42.5 reduce-scatter.1
where the time goes:
time: 634 us; the launch traced here: 630 us
  waiting for transfers between devices  502 us (79%)
  blocking collectives  89.5 us (14%)
  between operations  14.5 us (2%)
  local copies, waits for them, and re-layouts  12 us (2%)
  matrix products  10.3 us (2%)
    unnamed x5, waiting for transfers between devices  345 us
    all_gather x1, blocking collectives, on_device(): lax.all_gather(block_scales, 'dp', axis=0, tiled=True)  89.5 us
    all_gather x1, waiting for transfers between devices, on_device(): full_cot = lax.all_gather(cotangent, 'node', axis=1, tiled=True)  61.9 us
    all_gather x1, waiting for transfers between devices, on_device(): lax.all_gather(weight_codes, 'dp', axis=0, tiled=True)  50.4 us
    reduce_scatter x1, waiting for transfers between devices, on_device(): lax.psum_scatter(partial_value, 'node', scatter_dimension=1, tiled=True)  44.9 us
  transfers between devices with their start and end apart: 4, of which 4 were waited for; matrix products, arithmetic and copies ran while one was open for 3% of the time, Pallas kernels for 0%

commit v1 on v0

v1 whole, which is shorter than its diff:
```python
import functools
import math

import jax
import jax.numpy as jnp
from jax import lax
from jax.experimental import pallas as pl
from jax.experimental.pallas import tpu as pltpu
from jax.sharding import PartitionSpec as P

NX = 4
PIECES = 4
BF16, F32 = jnp.bfloat16, jnp.float32
MESH = pl.DeviceIdType.MESH


def kernel(ny, nz, nx, tok_ref, code_ref, scale_ref, cot_ref,
           val_ref, tg_ref, wg_ref,
           tok, tok_t, codes, scales, full, gat, tmp, w, part, rss, rsr,
           vout, tgout, mine, sibs, sibr, xs, xr, zs, zr, fs, fr, wgout,
           in_sem, out_sem, ag_s, ag_r, rs_s, rs_r,
           wz_s, wz_r, wx_s, wx_r, wc_s, wc_r,
           gc_s, gc_r, gx_s, gx_r, gz_s, gz_r, gf_s, gf_r):
    rows, feats = tok.shape
    cols = codes.shape[1]
    hops = ny // 2
    piece = rows // PIECES
    half = PIECES // 2
    mb = ny // 4
    inv = 1.0 / math.sqrt(rows * nz * nx * 2)

    y = lax.axis_index("node")
    dp = lax.axis_index("dp")
    c = lax.rem(dp, 2)
    x = lax.rem(dp // 2, nx)
    z = dp // (2 * nx)

    def at(zz, xx, cc):
        return ((zz * nx + xx) * 2 + cc, y)

    right, left = (dp, lax.rem(y + 1, ny)), (dp, lax.rem(y + ny - 1, ny))
    sibling = at(z, x, 1 - c)

    def remote(src, dst, s_sem, r_sem, dev):
        return pltpu.make_async_remote_copy(
            src_ref=src, dst_ref=dst, send_sem=s_sem, recv_sem=r_sem, device_id=dev, device_id_type=MESH)

    def loop(n, body):
        lax.fori_loop(0, n, lambda i, carry: (body(i), carry)[1], 0)

    cp_cot = pltpu.make_async_copy(cot_ref, full.at[0], in_sem.at[0])
    cp_code = pltpu.make_async_copy(code_ref, codes, in_sem.at[1])
    cp_scale = pltpu.make_async_copy(scale_ref, scales, in_sem.at[2])
    cp_tok = pltpu.make_async_copy(tok_ref, tok, in_sem.at[3])
    for cp in (cp_cot, cp_code, cp_scale, cp_tok):
        cp.start()

    barrier = pltpu.get_barrier_semaphore()

    def greet(dev):
        pl.semaphore_signal(barrier, inc=1, device_id=dev, device_id_type=MESH)

    greet(right)
    greet(left)
    greet(sibling)
    for j in range(1, nx):
        greet(at(z, lax.rem(x + j, nx), c))
    loop(nz - 1, lambda j: greet(at(lax.rem(z + j + 1, nz), x, c)))
    pl.semaphore_wait(barrier, 3 + nx - 1 + nz - 1)

    def ag(d, h, p):
        src, dst = (h - 1, h) if d == 0 else ((ny - h + 1) % ny, ny - h)
        span = pl.ds(pl.multiple_of(p * piece, piece), piece)
        return remote(full.at[src, span], full.at[dst, span], ag_s.at[d, h - 1, p], ag_r.at[d, h - 1, p],
                      right if d == 0 else left)

    def ag_first():
        loop(PIECES, lambda p: (ag(0, 1, p).start(), ag(1, 1, p).start()))

    def ag_hop(h):
        if h == hops:
            loop(half, lambda p: (ag(0, h, p).wait_recv(), ag(1, h, p + half).wait_recv()))
        elif h == hops - 1:
            def body(p):
                q = p + half
                ag(0, h, p).wait_recv()
                ag(0, h + 1, p).start()
                ag(1, h, q).wait_recv()
                ag(1, h + 1, q).start()
            loop(half, body)
            loop(half, lambda p: (ag(0, h, p + half).wait_recv(), ag(1, h, p).wait_recv()))
        else:
            def body(p):
                ag(0, h, p).wait_recv()
                ag(0, h + 1, p).start()
                ag(1, h, p).wait_recv()
                ag(1, h + 1, p).start()
            loop(PIECES, body)

    def ag_drain():
        for h in range(1, hops):
            loop(PIECES, lambda p: (ag(0, h, p).wait_send(), ag(1, h, p).wait_send()))
        loop(half, lambda p: (ag(0, hops, p).wait_send(), ag(1, hops, p + half).wait_send()))

    def wz(j):
        return remote(gat.at[c, x, z], gat.at[c, x, z], wz_s.at[j], wz_r.at[j],
                      at(lax.rem(z + j + 1, nz), x, c))

    def wx(j):
        return remote(gat.at[c, x], gat.at[c, x], wx_s.at[j], wx_r.at[j], at(z, lax.rem(x + j + 1, nx), c))

    def wc(j):
        xx = lax.rem(x - j + nx, nx)
        return remote(gat.at[c, xx], gat.at[c, xx], wc_s.at[j], wc_r.at[j], sibling)

    def w_first():
        scale = scales[...].astype(F32)
        block = cols // scale.shape[1]
        for b in range(scale.shape[1]):
            span = slice(b * block, (b + 1) * block)
            gat[c, x, z, :, span] = (codes[:, span].astype(F32) * scale[:, b:b + 1]).astype(BF16)
        loop(nz - 1, lambda j: wz(j).start())

    def w_along_x():
        def arrived(j):
            zz = lax.rem(z + nz - j - 1, nz)
            remote(gat.at[c, x, zz], gat.at[c, x, zz], wz_s.at[j], wz_r.at[j], sibling).wait_recv()
        loop(nz - 1, arrived)
        for j in range(nx - 1):
            wx(j).start()
        wc(0).start()

    def w_across():
        for j in range(1, nx):
            xx = lax.rem(x + nx - j, nx)
            remote(gat.at[c, xx], gat.at[c, xx], wx_s.at[j - 1], wx_r.at[j - 1], sibling).wait_recv()
            wc(j).start()

    def w_done():
        for j in range(nx):
            xx = lax.rem(x + nx - j, nx)
            remote(gat.at[1 - c, xx], gat.at[1 - c, xx], wc_s.at[j], wc_r.at[j], sibling).wait_recv()

        def lay(zz):
            for xx in range(nx):
                for cc in range(2):
                    at_row = 8 * xx + 4 * cc
                    tmp[at_row:at_row + 4, :] = gat[cc, xx, zz].astype(F32)
            n = 8 * nx
            w[pl.ds(pl.multiple_of(zz * n, n), n), :] = tmp[...].astype(BF16)
        loop(nz, lay)

    def w_drain():
        loop(nz - 1, lambda j: wz(j).wait_send())
        for j in range(nx - 1):
            wx(j).wait_send()
        for j in range(nx):
            wc(j).wait_send()

    tile = min(256, piece)

    def w_cols(k):
        owner = lax.rem(y + k, ny)
        return w[:, pl.ds(pl.multiple_of(owner * 128, 128), 128)]

    def partial(*ks):
        def body(i):
            span = pl.ds(pl.multiple_of(i * tile, tile), tile)
            rhs = jnp.concatenate([w_cols(k) for k in ks], axis=1)
            out = jnp.dot(tok[span, :], rhs, preferred_element_type=F32)
            for n, k in enumerate(ks):
                part[k, span, :] = out[:, n * 128:(n + 1) * 128]
        loop(rows // tile, body)

    def rs(d, t, p):
        span = pl.ds(pl.multiple_of(p * piece, piece), piece)
        return remote(rss.at[d, t - 1, span], rsr.at[d, t - 1, span], rs_s.at[d, t - 1, p], rs_r.at[d, t - 1, p],
                      right if d == 0 else left)

    def rs_send(d, t, p, arrives):
        s = hops - t + 1
        k = s if d == 0 else ny - s
        span = pl.ds(pl.multiple_of(p * piece, piece), piece)
        total = part[k, span, :]
        if arrives:
            rs(d, t - 1, p).wait_recv()
            total = total + rsr[d, t - 2, span, :].astype(F32)
        rss[d, t - 1, span, :] = total.astype(BF16)
        rs(d, t, p).start()

    def rs_first():
        loop(half, lambda p: (rs_send(0, 1, p, False), rs_send(1, 1, p + half, False)))

    def rs_second_own():
        loop(half, lambda p: (rs_send(0, 2, p + half, False), rs_send(1, 2, p, False)))

    def rs_second_sum():
        loop(half, lambda p: (rs_send(0, 2, p, True), rs_send(1, 2, p + half, True)))

    def rs_step(t, lo=0, hi=PIECES):
        def body(i):
            p = i + lo
            rs_send(0, t, lax.rem(p + half, PIECES), True)
            rs_send(1, t, p, True)
        loop(hi - lo, body)

    def rs_out(p):
        span = pl.ds(pl.multiple_of(p * piece, piece), piece)
        return pltpu.make_async_copy(vout.at[span], val_ref.at[span], out_sem.at[p])

    def rs_last():
        def body(i):
            rs(0, hops, lax.rem(i + half, PIECES)).wait_recv()
            rs(1, hops, i).wait_recv()
        loop(half, body)

        def fin(i):
            a, b = i, i + half
            rs(0, hops, a).wait_recv()
            rs(1, hops, b).wait_recv()
            for p in (a, b):
                span = pl.ds(pl.multiple_of(p * piece, piece), piece)
                total = part[0, span, :] + rsr[0, hops - 1, span, :].astype(F32) + rsr[1, hops - 1, span, :].astype(F32)
                vout[span, :] = total.astype(BF16)
                rs_out(p).start()
        loop(half, fin)

    def rs_drain():
        loop(half, lambda p: (rs(0, 1, p).wait_send(), rs(1, 1, p + half).wait_send()))
        for t in range(2, hops + 1):
            loop(PIECES, lambda p: (rs(0, t, p).wait_send(), rs(1, t, p).wait_send()))

    def token_grad(lo, hi):
        def body(i):
            span = pl.ds(pl.multiple_of((i + lo) * tile, tile), tile)
            lhs = jnp.concatenate([full[lax.rem(y + ny - k, ny), span, :] for k in range(ny)], axis=1)
            out = lax.dot_general(lhs, w[...], (((1,), (1,)), ((), ())), preferred_element_type=F32)
            tgout[span, :] = out.astype(BF16)
        loop(hi - lo, body)

    cp_tg = pltpu.make_async_copy(tgout, tg_ref, out_sem.at[PIECES])

    order = [0]
    for k in range(1, hops):
        order += [k, ny - k]
    order.append(hops)

    def slots(ph, cc):
        first = order[ph * 2 * mb:ph * 2 * mb + mb]
        second = order[ph * 2 * mb + mb:(ph + 1) * 2 * mb]
        return [jnp.where(cc == 0, a, b) for a, b in zip(first, second)]

    def wg_term(ph, cc, out):
        group = min(128, feats)
        per = group // (8 * nx)

        def body(i):
            rhs = jnp.concatenate([full[s] for s in slots(ph, cc)], axis=1)
            term = jnp.dot(tok_t[pl.ds(pl.multiple_of(i * group, group), group), :], rhs, preferred_element_type=F32)
            for u in range(per):
                for xx in range(nx):
                    for m in range(mb):
                        lo = (u * nx + xx) * 8
                        out[ph, xx, i * per + u, m] = term[lo:lo + 8, m * 128:(m + 1) * 128].astype(out.dtype)
        loop(feats // group, body)

    def gc(ph):
        return remote(sibs.at[ph], sibr.at[ph], gc_s.at[ph], gc_r.at[ph], sibling)

    def gx(ph, j):
        return remote(xs.at[ph, j], xr.at[ph, j], gx_s.at[ph, j], gx_r.at[ph, j], at(z, lax.rem(x + j + 1, nx), c))

    def gz(ph, j):
        zz = lax.rem(z + j + 1, nz)
        return remote(zs.at[ph, zz], zr.at[ph, j], gz_s.at[ph, j], gz_r.at[ph, j], at(zz, x, c))

    def gf(ph):
        return remote(fs.at[ph], fr.at[ph], gf_s.at[ph], gf_r.at[ph], sibling)

    def wg_first(ph):
        wg_term(ph, 1 - c, sibs)
        gc(ph).start()
        wg_term(ph, c, mine)

    def wg_along_x(ph):
        gc(ph).wait_recv()

        def body(zz):
            for j in range(nx):
                xx = lax.rem(x + j, nx)
                total = mine[ph, xx, zz] + sibr[ph, xx, zz].astype(F32)
                if j == 0:
                    mine[ph, xx, zz] = total
                else:
                    xs[ph, j - 1, zz] = total.astype(BF16)
        loop(nz, body)
        for j in range(nx - 1):
            gx(ph, j).start()

    def wg_along_z(ph):
        for j in range(nx - 1):
            gx(ph, j).wait_recv()

        def body(zz):
            total = mine[ph, x, zz]
            for j in range(nx - 1):
                total = total + xr[ph, j, zz].astype(F32)
            mine[ph, x, zz] = total
            zs[ph, zz] = total.astype(BF16)
        loop(nz, body)
        loop(nz - 1, lambda j: gz(ph, j).start())

    def place(ph, cc, value):
        for m, s in enumerate(slots(ph, cc)):
            col = lax.rem(y + ny - s, ny) * 128
            wgout[:, pl.ds(pl.multiple_of(col, 128), 128)] = value[m]

    def wg_across(ph):
        loop(nz - 1, lambda j: gz(ph, j).wait_recv())
        total = mine[ph, x, z]
        for j in range(nz - 1):
            total = total + zr[ph, j].astype(F32)
        total = total * F32(inv)
        low, high = total[:, :4, :], total[:, 4:, :]
        fs[ph] = jnp.where(c == 0, high, low)
        gf(ph).start()
        place(ph, c, jnp.where(c == 0, low, high))

    cp_wg = pltpu.make_async_copy(wgout, wg_ref, out_sem.at[PIECES + 1])

    def wg_last():
        for ph in range(2):
            gf(ph).wait_recv()
            place(ph, 1 - c, fr[ph])
        cp_wg.start()

    def wg_drain():
        for ph in range(2):
            gc(ph).wait_send()
            for j in range(nx - 1):
                gx(ph, j).wait_send()
            loop(nz - 1, lambda j: gz(ph, j).wait_send())
            gf(ph).wait_send()

    def turn():
        step = min(256, rows)

        def body(i):
            span = pl.ds(pl.multiple_of(i * step, step), step)
            tok_t[:, span] = tok[span, :].T
        loop(rows // step, body)

    cp_cot.wait()
    ag_first()
    cp_code.wait()
    cp_scale.wait()
    w_first()
    cp_tok.wait()
    turn()
    ag_hop(1)
    w_along_x()
    for h in range(2, hops - 1):
        ag_hop(h)
    w_across()
    wg_first(0)
    ag_hop(hops - 1)
    wg_along_x(0)
    w_done()
    partial(hops)
    rs_first()
    ag_hop(hops)
    partial(hops - 1, hops + 1)
    rs_second_own()
    wg_along_z(0)
    wg_first(1)
    for k in range(hops - 2, 0, -1):
        partial(k, ny - k)
    rs_second_sum()
    wg_along_x(1)
    partial(0)
    wg_across(0)
    if hops > 2:
        rs_step(3)
    wg_along_z(1)
    token_grad(0, rows // tile // 2)
    for t in range(4, hops + 1):
        rs_step(t)
    wg_across(1)
    token_grad(rows // tile // 2, rows // tile)
    cp_tg.start()
    wg_last()
    rs_last()
    ag_drain()
    w_drain()
    wg_drain()
    rs_drain()
    loop(PIECES, lambda p: rs_out(p).wait())
    cp_tg.wait()
    cp_wg.wait()


def on_device(ny, nz, nx, tokens, codes, scales, cot):
    rows, feats = tokens.shape
    cols = codes.shape[1]
    hops, mb = ny // 2, ny // 4
    any_ = pl.BlockSpec(memory_space=pl.ANY)
    dma = pltpu.SemaphoreType.DMA
    v = pltpu.VMEM
    scratch = [
        v((rows, feats), BF16), v((feats, rows), BF16), v(codes.shape, BF16), v(scales.shape, BF16),
        v((ny, rows, 128), BF16), v((2, nx, nz, 4, cols), BF16), v((8 * nx, cols), F32), v((feats, cols), BF16),
        v((ny, rows, 128), F32), v((2, hops, rows, 128), BF16), v((2, hops, rows, 128), BF16),
        v((rows, 128), BF16), v((rows, feats), BF16),
        v((2, nx, nz, mb, 8, 128), F32), v((2, nx, nz, mb, 8, 128), BF16), v((2, nx, nz, mb, 8, 128), BF16),
        v((2, nx - 1, nz, mb, 8, 128), BF16), v((2, nx - 1, nz, mb, 8, 128), BF16),
        v((2, nz, mb, 8, 128), BF16), v((2, nz - 1, mb, 8, 128), BF16),
        v((2, mb, 4, 128), F32), v((2, mb, 4, 128), F32), v((4, cols), F32),
        dma((4,)), dma((PIECES + 2,)),
        dma((2, hops, PIECES)), dma((2, hops, PIECES)), dma((2, hops, PIECES)), dma((2, hops, PIECES)),
        dma((nz - 1,)), dma((nz - 1,)), dma((nx - 1,)), dma((nx - 1,)), dma((nx,)), dma((nx,)),
        dma((2,)), dma((2,)), dma((2, nx - 1)), dma((2, nx - 1)), dma((2, nz - 1)), dma((2, nz - 1)),
        dma((2,)), dma((2,)),
    ]
    flops = 6 * rows * feats * cols
    return pl.pallas_call(
        functools.partial(kernel, ny, nz, nx),
        out_shape=(
            jax.ShapeDtypeStruct((rows, 128), BF16),
            jax.ShapeDtypeStruct((rows, feats), BF16),
            jax.ShapeDtypeStruct((4, cols), F32),
        ),
        in_specs=[any_] * 4,
        out_specs=(any_,) * 3,
        scratch_shapes=scratch,
        compiler_params=pltpu.CompilerParams(
            collective_id=0, has_side_effects=True, vmem_limit_bytes=56 * 2**20),
        cost_estimate=pl.CostEstimate(flops=flops, bytes_accessed=4 * rows * feats, transcendentals=0),
    )(tokens, codes, scales, cot)


def build(mesh, nx):
    ny = mesh.shape["node"]
    nz = mesh.shape["dp"] // (2 * nx)
    placed = (P("dp", "node"), P(("node", "dp"), None), P(("node", "dp"), None), P("dp", "node"))
    return jax.shard_map(
        functools.partial(on_device, ny, nz, nx),
        mesh=mesh,
        in_specs=placed,
        out_specs=(P("dp", "node"), P("dp", "node"), P(("node", "dp"), None)),
        check_vma=False,
    )


def solution(mesh):
    return build(mesh, NX)
```

time: 634 us -> 76.8 us (0.12)
  waiting for transfers between devices: 502 us -> 0 us
  blocking collectives: 89.5 us -> 0 us
  Pallas kernels: 0 us -> 71.4 us
  between operations: 14.5 us -> 0.64 us
  matrix products: 10.3 us -> 0 us
  local copies, waits for them, and re-layouts: 12 us -> 4.55 us
    unnamed x5 -> x0, waiting for transfers between devices: 345 us -> none
    all_gather x2 -> x0, waiting for transfers between devices: 112 us -> none  [the longest x1 61.9 us: on_device(): full_cot = lax.all_gather(cotangent, 'node', axis=1, tiled=True)]
    all_gather x1 -> x0, blocking collectives: 89.5 us -> none  [on_device(): lax.all_gather(block_scales, 'dp', axis=0, tiled=True)]
    pallas_call x0 -> x1, Pallas kernels: none -> 71.4 us  [on_device(): pl.pallas_call(functools.partial(kernel, ny, nz, nx), out_shape=(jax.Shap...]
    reduce_scatter x1 -> x0, waiting for transfers between devices: 44.9 us -> none  [on_device(): lax.psum_scatter(partial_value, 'node', scatter_dimension=1, tiled=True)]
    dot_general x3 -> x0, matrix products: 10.3 us -> none  [the longest x1 4.18 us: on_device(): lax.dot_general(tokens, full_cot, (((0,), (0,)), ((), ())), preferred_ele...]
  transfers between devices with their start and end apart: 4 -> 0, of which waited for: 4 -> 0; matrix products, arithmetic and copies ran while one was open for 3% -> 0% of each run, Pallas kernels for 0% -> 0%
where the time goes in v1:
time: 76.8 us; the launch traced here: 76.6 us
  Pallas kernels  71.4 us (93%)
  local copies, waits for them, and re-layouts  4.55 us (6%)
    pallas_call x1, Pallas kernels, on_device(): pl.pallas_call(functools.partial(kernel, ny, nz, nx), out_shape=(jax.Shap...  71.4 us
    unnamed x5, local copies, waits for them, and re-layouts  4.55 us

profile of v1, /device:TPU:1, one launch (start us, length us, event | category | flops | bytes accessed | tf_op | source)
XLA Modules:
  0.0 76.6 jit_solution(16050483823519352602)
XLA Ops:
  0.6 71.4 %shard_map.67 = (bf16[1024,128]{1,0:T(8,128)(2,1)}, bf16[1024,512]{1,0:T(8,128)(2,1)}, f32[4,1024]{1,0:T(4,128)}) custom-call(bf16[1024,512]{1,0:T(8,128)(2,1)} %tok_ref.1, bf16[4,1024]{1,0:T(4,128)(2,1)} %code_ref.1, bf16[4,4]{1,0:T(4,128)(2,1)} %scale_ref.1, bf16[1024,128]{1,0:T(8,128)(2,1)} %cot_ref.1), custom_call_target="tpu_custom_call" | custom-call | flops 3221225472 | bytes 2097152 | tf_op jit(solution)/shard_map/pallas_call | solution.py:425
  72.1 1.7 %copy.10 = bf16[1024,128]{1,0:T(8,128)(2,1)} copy(bf16[1024,128]{1,0:T(8,128)(2,1)} %get-tuple-element.6) | data formatting | bytes 524288
  73.7 0.0 copy-start
  73.7 2.3 %copy.11 = bf16[1024,512]{1,0:T(8,128)(2,1)} copy(bf16[1024,512]{1,0:T(8,128)(2,1)} %get-tuple-element.7) | data formatting | bytes 2097152
  76.0 0.0 copy-done
  76.0 0.6 copy.12
Async XLA Ops:
  73.7 2.3 %copy-start = (f32[4,1024]{1,0:T(4,128)S(1)}, f32[4,1024]{1,0:T(4,128)}, u32[]{:S(2)}) copy-start(f32[4,1024]{1,0:T(4,128)} %get-tuple-element.8) | copy-start | bytes 49156

commit v2 on v1

--- a/solution.py
+++ b/solution.py
@@ -15,10 +15,10 @@
 
 
 def kernel(ny, nz, nx, tok_ref, code_ref, scale_ref, cot_ref,
-           val_ref, tg_ref, wg_ref,
+           vout, tgout, wgout,
            tok, tok_t, codes, scales, full, gat, tmp, w, part, rss, rsr,
-           vout, tgout, mine, sibs, sibr, xs, xr, zs, zr, fs, fr, wgout,
-           in_sem, out_sem, ag_s, ag_r, rs_s, rs_r,
+           mine, sibs, sibr, xs, xr, zs, zr, fs, fr,
+           in_sem, ag_s, ag_r, rs_s, rs_r,
            wz_s, wz_r, wx_s, wx_r, wc_s, wc_r,
            gc_s, gc_r, gx_s, gx_r, gz_s, gz_r, gf_s, gf_r):
     rows, feats = tok.shape
@@ -197,22 +197,17 @@
     def rs_second_sum():
         loop(half, lambda p: (rs_send(0, 2, p, True), rs_send(1, 2, p + half, True)))
 
-    def rs_step(t, lo=0, hi=PIECES):
+    def rs_step(t, late):
         def body(i):
-            p = i + lo
-            rs_send(0, t, lax.rem(p + half, PIECES), True)
-            rs_send(1, t, p, True)
-        loop(hi - lo, body)
-
-    def rs_out(p):
-        span = pl.ds(pl.multiple_of(p * piece, piece), piece)
-        return pltpu.make_async_copy(vout.at[span], val_ref.at[span], out_sem.at[p])
+            rs_send(0, t, i + (0 if late else half), True)
+            rs_send(1, t, i + (half if late else 0), True)
+        loop(half, body)
 
     def rs_last():
-        def body(i):
-            rs(0, hops, lax.rem(i + half, PIECES)).wait_recv()
+        def seen(i):
+            rs(0, hops, i + half).wait_recv()
             rs(1, hops, i).wait_recv()
-        loop(half, body)
+        loop(half, seen)
 
         def fin(i):
             a, b = i, i + half
@@ -222,7 +217,6 @@
                 span = pl.ds(pl.multiple_of(p * piece, piece), piece)
                 total = part[0, span, :] + rsr[0, hops - 1, span, :].astype(F32) + rsr[1, hops - 1, span, :].astype(F32)
                 vout[span, :] = total.astype(BF16)
-                rs_out(p).start()
         loop(half, fin)
 
     def rs_drain():
@@ -237,8 +231,6 @@
             out = lax.dot_general(lhs, w[...], (((1,), (1,)), ((), ())), preferred_element_type=F32)
             tgout[span, :] = out.astype(BF16)
         loop(hi - lo, body)
-
-    cp_tg = pltpu.make_async_copy(tgout, tg_ref, out_sem.at[PIECES])
 
     order = [0]
     for k in range(1, hops):
@@ -277,9 +269,11 @@
     def gf(ph):
         return remote(fs.at[ph], fr.at[ph], gf_s.at[ph], gf_r.at[ph], sibling)
 
-    def wg_first(ph):
+    def wg_theirs(ph):
         wg_term(ph, 1 - c, sibs)
         gc(ph).start()
+
+    def wg_mine(ph):
         wg_term(ph, c, mine)
 
     def wg_along_x(ph):
@@ -326,13 +320,10 @@
         gf(ph).start()
         place(ph, c, jnp.where(c == 0, low, high))
 
-    cp_wg = pltpu.make_async_copy(wgout, wg_ref, out_sem.at[PIECES + 1])
-
     def wg_last():
         for ph in range(2):
             gf(ph).wait_recv()
             place(ph, 1 - c, fr[ph])
-        cp_wg.start()
 
     def wg_drain():
         for ph in range(2):
@@ -361,8 +352,9 @@
     w_along_x()
     for h in range(2, hops - 1):
         ag_hop(h)
+    wg_theirs(0)
+    wg_mine(0)
     w_across()
-    wg_first(0)
     ag_hop(hops - 1)
     wg_along_x(0)
     w_done()
@@ -371,72 +363,64 @@
     ag_hop(hops)
     partial(hops - 1, hops + 1)
     rs_second_own()
+    wg_theirs(1)
     wg_along_z(0)
-    wg_first(1)
-    for k in range(hops - 2, 0, -1):
-        partial(k, ny - k)
     rs_second_sum()
+    wg_mine(1)
+    partial(2, ny - 2)
     wg_along_x(1)
+    rs_step(3, False)
+    partial(1, ny - 1)
+    wg_across(0)
+    rs_step(3, True)
+    wg_along_z(1)
+    rs_step(4, False)
     partial(0)
-    wg_across(0)
-    if hops > 2:
-        rs_step(3)
-    wg_along_z(1)
     token_grad(0, rows // tile // 2)
-    for t in range(4, hops + 1):
-        rs_step(t)
+    rs_step(4, True)
+    token_grad(rows // tile // 2, rows // tile)
+    rs_last()
     wg_across(1)
-    token_grad(rows // tile // 2, rows // tile)
-    cp_tg.start()
     wg_last()
-    rs_last()
     ag_drain()
     w_drain()
     wg_drain()
     rs_drain()
-    loop(PIECES, lambda p: rs_out(p).wait())
-    cp_tg.wait()
-    cp_wg.wait()
 
 
 def on_device(ny, nz, nx, tokens, codes, scales, cot):
     rows, feats = tokens.shape
     cols = codes.shape[1]
     hops, mb = ny // 2, ny // 4
-    any_ = pl.BlockSpec(memory_space=pl.ANY)
+    hbm = pl.BlockSpec(memory_space=pltpu.HBM)
     dma = pltpu.SemaphoreType.DMA
     v = pltpu.VMEM
     scratch = [
         v((rows, feats), BF16), v((feats, rows), BF16), v(codes.shape, BF16), v(scales.shape, BF16),
         v((ny, rows, 128), BF16), v((2, nx, nz, 4, cols), BF16), v((8 * nx, cols), F32), v((feats, cols), BF16),
         v((ny, rows, 128), F32), v((2, hops, rows, 128), BF16), v((2, hops, rows, 128), BF16),
-        v((rows, 128), BF16), v((rows, feats), BF16),
         v((2, nx, nz, mb, 8, 128), F32), v((2, nx, nz, mb, 8, 128), BF16), v((2, nx, nz, mb, 8, 128), BF16),
         v((2, nx - 1, nz, mb, 8, 128), BF16), v((2, nx - 1, nz, mb, 8, 128), BF16),
         v((2, nz, mb, 8, 128), BF16), v((2, nz - 1, mb, 8, 128), BF16),
-        v((2, mb, 4, 128), F32), v((2, mb, 4, 128), F32), v((4, cols), F32),
-        dma((4,)), dma((PIECES + 2,)),
+        v((2, mb, 4, 128), F32), v((2, mb, 4, 128), F32),
+        dma((4,)),
         dma((2, hops, PIECES)), dma((2, hops, PIECES)), dma((2, hops, PIECES)), dma((2, hops, PIECES)),
         dma((nz - 1,)), dma((nz - 1,)), dma((nx - 1,)), dma((nx - 1,)), dma((nx,)), dma((nx,)),
         dma((2,)), dma((2,)), dma((2, nx - 1)), dma((2, nx - 1)), dma((2, nz - 1)), dma((2, nz - 1)),
         dma((2,)), dma((2,)),
     ]
     flops = 6 * rows * feats * cols
+    shapes = (((rows, 128), BF16), ((rows, feats), BF16), ((4, cols), F32))
     return pl.pallas_call(
         functools.partial(kernel, ny, nz, nx),
-        out_shape=(
-            jax.ShapeDtypeStruct((rows, 128), BF16),
-            jax.ShapeDtypeStruct((rows, feats), BF16),
-            jax.ShapeDtypeStruct((4, cols), F32),
-        ),
-        in_specs=[any_] * 4,
-        out_specs=(any_,) * 3,
+        out_shape=tuple(v(shape, dtype) for shape, dtype in shapes),
+        in_specs=[hbm] * 4,
+        out_specs=(pl.BlockSpec(memory_space=v),) * 3,
         scratch_shapes=scratch,
         compiler_params=pltpu.CompilerParams(
-            collective_id=0, has_side_effects=True, vmem_limit_bytes=56 * 2**20),
+            collective_id=0, has_side_effects=True, vmem_limit_bytes=61 * 2**20),
         cost_estimate=pl.CostEstimate(flops=flops, bytes_accessed=4 * rows * feats, transcendentals=0),
     )(tokens, codes, scales, cot)
-
 
 def build(mesh, nx):
     ny = mesh.shape["node"]

time: 76.8 us -> 72.9 us (0.949)
  local copies, waits for them, and re-layouts: 4.55 us -> 2.28 us
  Pallas kernels: 71.4 us -> 69.9 us
    unnamed x5 -> x3, local copies, waits for them, and re-layouts: 4.55 us -> 2.28 us
    pallas_call x1, Pallas kernels: 71.4 us -> 69.9 us  [on_device(): pl.pallas_call(functools.partial(kernel, ny, nz, nx), out_shape=tuple((v(...]
where the time goes in v2:
time: 72.9 us; the launch traced here: 72.8 us
  Pallas kernels  69.9 us (96%)
  local copies, waits for them, and re-layouts  2.28 us (3%)
    pallas_call x1, Pallas kernels, on_device(): pl.pallas_call(functools.partial(kernel, ny, nz, nx), out_shape=tuple((v(...  69.9 us
    unnamed x3, local copies, waits for them, and re-layouts  2.28 us

profile of v2, /device:TPU:1, one launch (start us, length us, event | category | flops | bytes accessed | tf_op | source)
XLA Modules:
  0.0 72.8 jit_solution(1974233246165267048)
XLA Ops:
  0.6 69.9 %shard_map.67 = (bf16[1024,128]{1,0:T(8,128)(2,1)S(1)}, bf16[1024,512]{1,0:T(8,128)(2,1)S(1)}, f32[4,1024]{1,0:T(4,128)S(1)}) custom-call(bf16[1024,512]{1,0:T(8,128)(2,1)} %tok_ref.1, bf16[4,1024]{1,0:T(4,128)(2,1)} %code_ref.1, bf16[4,4]{1,0:T(4,128)(2,1)} %scale_ref.1, bf16[1024,128]{1,0:T(8,128)(2,1)} %cot_ref.1), custom_call_target="tpu_custom_call" | custom-call | flops 3221225472 | bytes 2097152 | tf_op jit(solution)/shard_map/pallas_call | solution.py:414
  70.5 0.7 copy.10
  71.2 0.6 copy.12
  71.8 1.0 %copy.11 = bf16[1024,512]{1,0:T(8,128)(2,1)} copy(bf16[1024,512]{1,0:T(8,128)(2,1)S(1)} %get-tuple-element.4) | data formatting | bytes 2097152

commit v3 on v2

--- a/solution.py
+++ b/solution.py
@@ -14,10 +14,14 @@
 MESH = pl.DeviceIdType.MESH
 
 
+def phases(ny):
+    return ny // 4, ny // 4
+
+
 def kernel(ny, nz, nx, tok_ref, code_ref, scale_ref, cot_ref,
            vout, tgout, wgout,
            tok, tok_t, codes, scales, full, gat, tmp, w, part, rss, rsr,
-           mine, sibs, sibr, xs, xr, zs, zr, fs, fr,
+           mine0, sibs0, sibr0, xs0, xr0, zs0, zr0, fs0, fr0, mine1, sibs1, sibr1, xs1, xr1, zs1, zr1, fs1, fr1,
            in_sem, ag_s, ag_r, rs_s, rs_r,
            wz_s, wz_r, wx_s, wx_r, wc_s, wc_r,
            gc_s, gc_r, gx_s, gx_r, gz_s, gz_r, gf_s, gf_r):
@@ -26,7 +30,9 @@
     hops = ny // 2
     piece = rows // PIECES
     half = PIECES // 2
-    mb = ny // 4
+    sizes = phases(ny)
+    mine, sibs, sibr, xs, xr = (mine0, mine1), (sibs0, sibs1), (sibr0, sibr1), (xs0, xs1), (xr0, xr1)
+    zs, zr, fs, fr = (zs0, zs1), (zr0, zr1), (fs0, fs1), (fr0, fr1)
     inv = 1.0 / math.sqrt(rows * nz * nx * 2)
 
     y = lax.axis_index("node")
@@ -47,6 +53,12 @@
 
     def loop(n, body):
         lax.fori_loop(0, n, lambda i, carry: (body(i), carry)[1], 0)
+
+    def far_first(body):
+        def one(k):
+            near = (k + 1) // 2
+            body(nz // 2 - 1 + jnp.where(lax.rem(k, 2) == 0, near, -near))
+        loop(nz - 1, one)
 
     cp_cot = pltpu.make_async_copy(cot_ref, full.at[0], in_sem.at[0])
     cp_code = pltpu.make_async_copy(code_ref, codes, in_sem.at[1])
@@ -65,7 +77,7 @@
     greet(sibling)
     for j in range(1, nx):
         greet(at(z, lax.rem(x + j, nx), c))
-    loop(nz - 1, lambda j: greet(at(lax.rem(z + j + 1, nz), x, c)))
+    far_first(lambda j: greet(at(lax.rem(z + j + 1, nz), x, c)))
     pl.semaphore_wait(barrier, 3 + nx - 1 + nz - 1)
 
     def ag(d, h, p):
@@ -119,7 +131,7 @@
         for b in range(scale.shape[1]):
             span = slice(b * block, (b + 1) * block)
             gat[c, x, z, :, span] = (codes[:, span].astype(F32) * scale[:, b:b + 1]).astype(BF16)
-        loop(nz - 1, lambda j: wz(j).start())
+        far_first(lambda j: wz(j).start())
 
     def w_along_x():
         def arrived(j):
@@ -238,12 +250,12 @@
     order.append(hops)
 
     def slots(ph, cc):
-        first = order[ph * 2 * mb:ph * 2 * mb + mb]
-        second = order[ph * 2 * mb + mb:(ph + 1) * 2 * mb]
+        mb, start = sizes[ph], 2 * sum(sizes[:ph])
+        first, second = order[start:start + mb], order[start + mb:start + 2 * mb]
         return [jnp.where(cc == 0, a, b) for a, b in zip(first, second)]
 
     def wg_term(ph, cc, out):
-        group = min(128, feats)
+        group, mb = min(128, feats), sizes[ph]
         per = group // (8 * nx)
 
         def body(i):
@@ -253,21 +265,21 @@
                 for xx in range(nx):
                     for m in range(mb):
                         lo = (u * nx + xx) * 8
-                        out[ph, xx, i * per + u, m] = term[lo:lo + 8, m * 128:(m + 1) * 128].astype(out.dtype)
+                        out[ph][xx, i * per + u, m] = term[lo:lo + 8, m * 128:(m + 1) * 128].astype(out[ph].dtype)
         loop(feats // group, body)
 
     def gc(ph):
-        return remote(sibs.at[ph], sibr.at[ph], gc_s.at[ph], gc_r.at[ph], sibling)
+        return remote(sibs[ph], sibr[ph], gc_s.at[ph], gc_r.at[ph], sibling)
 
     def gx(ph, j):
-        return remote(xs.at[ph, j], xr.at[ph, j], gx_s.at[ph, j], gx_r.at[ph, j], at(z, lax.rem(x + j + 1, nx), c))
+        return remote(xs[ph].at[j], xr[ph].at[j], gx_s.at[ph, j], gx_r.at[ph, j], at(z, lax.rem(x + j + 1, nx), c))
 
     def gz(ph, j):
         zz = lax.rem(z + j + 1, nz)
-        return remote(zs.at[ph, zz], zr.at[ph, j], gz_s.at[ph, j], gz_r.at[ph, j], at(zz, x, c))
+        return remote(zs[ph].at[zz], zr[ph].at[j], gz_s.at[ph, j], gz_r.at[ph, j], at(zz, x, c))
 
     def gf(ph):
-        return remote(fs.at[ph], fr.at[ph], gf_s.at[ph], gf_r.at[ph], sibling)
+        return remote(fs[ph], fr[ph], gf_s.at[ph], gf_r.at[ph], sibling)
 
     def wg_theirs(ph):
         wg_term(ph, 1 - c, sibs)
@@ -282,11 +294,11 @@
         def body(zz):
             for j in range(nx):
                 xx = lax.rem(x + j, nx)
-                total = mine[ph, xx, zz] + sibr[ph, xx, zz].astype(F32)
+                total = mine[ph][xx, zz] + sibr[ph][xx, zz].astype(F32)
                 if j == 0:
-                    mine[ph, xx, zz] = total
+                    mine[ph][xx, zz] = total
                 else:
-                    xs[ph, j - 1, zz] = total.astype(BF16)
+                    xs[ph][j - 1, zz] = total.astype(BF16)
         loop(nz, body)
         for j in range(nx - 1):
             gx(ph, j).start()
@@ -296,13 +308,13 @@
             gx(ph, j).wait_recv()
 
         def body(zz):
-            total = mine[ph, x, zz]
+            total = mine[ph][x, zz]
             for j in range(nx - 1):
-                total = total + xr[ph, j, zz].astype(F32)
-            mine[ph, x, zz] = total
-            zs[ph, zz] = total.astype(BF16)
+                total = total + xr[ph][j, zz].astype(F32)
+            mine[ph][x, zz] = total
+            zs[ph][zz] = total.astype(BF16)
         loop(nz, body)
-        loop(nz - 1, lambda j: gz(ph, j).start())
+        far_first(lambda j: gz(ph, j).start())
 
     def place(ph, cc, value):
         for m, s in enumerate(slots(ph, cc)):
@@ -311,19 +323,19 @@
 
     def wg_across(ph):
         loop(nz - 1, lambda j: gz(ph, j).wait_recv())
-        total = mine[ph, x, z]
+        total = mine[ph][x, z]
         for j in range(nz - 1):
-            total = total + zr[ph, j].astype(F32)
+            total = total + zr[ph][j].astype(F32)
         total = total * F32(inv)
         low, high = total[:, :4, :], total[:, 4:, :]
-        fs[ph] = jnp.where(c == 0, high, low)
+        fs[ph][...] = jnp.where(c == 0, high, low)
         gf(ph).start()
         place(ph, c, jnp.where(c == 0, low, high))
 
     def wg_last():
         for ph in range(2):
             gf(ph).wait_recv()
-            place(ph, 1 - c, fr[ph])
+            place(ph, 1 - c, fr[ph][...])
 
     def wg_drain():
         for ph in range(2):
@@ -356,31 +368,31 @@
     wg_mine(0)
     w_across()
     ag_hop(hops - 1)
-    wg_along_x(0)
     w_done()
     partial(hops)
     rs_first()
+    wg_along_x(0)
     ag_hop(hops)
+    wg_theirs(1)
+    wg_mine(1)
     partial(hops - 1, hops + 1)
     rs_second_own()
-    wg_theirs(1)
+    wg_along_x(1)
+    rs_second_sum()
     wg_along_z(0)
-    rs_second_sum()
-    wg_mine(1)
     partial(2, ny - 2)
-    wg_along_x(1)
     rs_step(3, False)
+    wg_along_z(1)
     partial(1, ny - 1)
+    rs_step(3, True)
     wg_across(0)
-    rs_step(3, True)
-    wg_along_z(1)
     rs_step(4, False)
     partial(0)
     token_grad(0, rows // tile // 2)
     rs_step(4, True)
     token_grad(rows // tile // 2, rows // tile)
+    wg_across(1)
     rs_last()
-    wg_across(1)
     wg_last()
     ag_drain()
     w_drain()
@@ -388,10 +400,21 @@
     rs_drain()
 
 
+def deliver(a, b, d, a_out, b_out, d_out, sem):
+    half = b.shape[0] // 2
+    top, low = pl.ds(0, half), pl.ds(half, half)
+    pairs = ((b.at[top], b_out.at[top]), (b.at[low], b_out.at[low]), (a, a_out), (d, d_out))
+    copies = [pltpu.make_async_copy(src, dst, sem.at[i]) for i, (src, dst) in enumerate(pairs)]
+    for cp in copies:
+        cp.start()
+    for cp in copies:
+        cp.wait()
+
+
 def on_device(ny, nz, nx, tokens, codes, scales, cot):
     rows, feats = tokens.shape
     cols = codes.shape[1]
-    hops, mb = ny // 2, ny // 4
+    hops = ny // 2
     hbm = pl.BlockSpec(memory_space=pltpu.HBM)
     dma = pltpu.SemaphoreType.DMA
     v = pltpu.VMEM
@@ -399,10 +422,11 @@
         v((rows, feats), BF16), v((feats, rows), BF16), v(codes.shape, BF16), v(scales.shape, BF16),
         v((ny, rows, 128), BF16), v((2, nx, nz, 4, cols), BF16), v((8 * nx, cols), F32), v((feats, cols), BF16),
         v((ny, rows, 128), F32), v((2, hops, rows, 128), BF16), v((2, hops, rows, 128), BF16),
-        v((2, nx, nz, mb, 8, 128), F32), v((2, nx, nz, mb, 8, 128), BF16), v((2, nx, nz, mb, 8, 128), BF16),
-        v((2, nx - 1, nz, mb, 8, 128), BF16), v((2, nx - 1, nz, mb, 8, 128), BF16),
-        v((2, nz, mb, 8, 128), BF16), v((2, nz - 1, mb, 8, 128), BF16),
-        v((2, mb, 4, 128), F32), v((2, mb, 4, 128), F32),
+        *(shape for mb in phases(ny) for shape in (
+            v((nx, nz, mb, 8, 128), F32), v((nx, nz, mb, 8, 128), BF16), v((nx, nz, mb, 8, 128), BF16),
+            v((nx - 1, nz, mb, 8, 128), BF16), v((nx - 1, nz, mb, 8, 128), BF16),
+            v((nz, mb, 8, 128), BF16), v((nz - 1, mb, 8, 128), BF16),
+            v((mb, 4, 128), F32), v((mb, 4, 128), F32))),
         dma((4,)),
         dma((2, hops, PIECES)), dma((2, hops, PIECES)), dma((2, hops, PIECES)), dma((2, hops, PIECES)),
         dma((nz - 1,)), dma((nz - 1,)), dma((nx - 1,)), dma((nx - 1,)), dma((nx,)), dma((nx,)),
@@ -411,7 +435,7 @@
     ]
     flops = 6 * rows * feats * cols
     shapes = (((rows, 128), BF16), ((rows, feats), BF16), ((4, cols), F32))
-    return pl.pallas_call(
+    results = pl.pallas_call(
         functools.partial(kernel, ny, nz, nx),
         out_shape=tuple(v(shape, dtype) for shape, dtype in shapes),
         in_specs=[hbm] * 4,
@@ -421,6 +445,15 @@
             collective_id=0, has_side_effects=True, vmem_limit_bytes=61 * 2**20),
         cost_estimate=pl.CostEstimate(flops=flops, bytes_accessed=4 * rows * feats, transcendentals=0),
     )(tokens, codes, scales, cot)
+    return pl.pallas_call(
+        deliver,
+        out_shape=tuple(jax.ShapeDtypeStruct(shape, dtype) for shape, dtype in shapes),
+        in_specs=[pl.BlockSpec(memory_space=v)] * 3,
+        out_specs=(hbm,) * 3,
+        scratch_shapes=[dma((4,))],
+        compiler_params=pltpu.CompilerParams(vmem_limit_bytes=2**20),
+        cost_estimate=pl.CostEstimate(flops=0, bytes_accessed=4 * rows * feats, transcendentals=0),
+    )(*(pltpu.with_memory_space_constraint(r, v) for r in results))
 
 def build(mesh, nx):
     ny = mesh.shape["node"]

time: 72.9 us -> 69.3 us (0.951); the launches traced: 72.8 us -> 68.1 us
  Pallas kernels: 69.9 us -> 67.5 us
  local copies, waits for them, and re-layouts: 2.28 us -> 0 us
    pallas_call x1, Pallas kernels: 69.9 us -> 66.4 us  [on_device(): pl.pallas_call(functools.partial(kernel, ny, nz, nx), out_shape=tuple((v(...]
    unnamed x3 -> x0, local copies, waits for them, and re-layouts: 2.28 us -> none
    pallas_call x0 -> x1, Pallas kernels: none -> 1.09 us  [on_device(): pl.pallas_call(deliver, out_shape=tuple((jax.ShapeDtypeStruct(shape, dtyp...]
where the time goes in v3:
time: 69.3 us; the launch traced here: 68.1 us
  Pallas kernels  67.5 us (97%)
    pallas_call x1, Pallas kernels, on_device(): pl.pallas_call(functools.partial(kernel, ny, nz, nx), out_shape=tuple((v(...  66.4 us

profile of v3, /device:TPU:1, one launch (start us, length us, event | category | flops | bytes accessed | tf_op | source)
XLA Modules:
  0.0 68.1 jit_solution(8954689169210740553)
XLA Ops:
  0.6 66.4 %shard_map.67 = (bf16[1024,128]{1,0:T(8,128)(2,1)S(1)}, bf16[1024,512]{1,0:T(8,128)(2,1)S(1)}, f32[4,1024]{1,0:T(4,128)S(1)}) custom-call(bf16[1024,512]{1,0:T(8,128)(2,1)} %tok_ref.1, bf16[4,1024]{1,0:T(4,128)(2,1)} %code_ref.1, bf16[4,4]{1,0:T(4,128)(2,1)} %scale_ref.1, bf16[1024,128]{1,0:T(8,128)(2,1)} %cot_ref.1), custom_call_target="tpu_custom_call" | custom-call | flops 3221225472 | bytes 2097152 | tf_op jit(solution)/shard_map/pallas_call | solution.py:438
  67.1 1.1 %shard_map.68 = (bf16[1024,128]{1,0:T(8,128)(2,1)}, bf16[1024,512]{1,0:T(8,128)(2,1)}, f32[4,1024]{1,0:T(4,128)}) custom-call(bf16[1024,128]{1,0:T(8,128)(2,1)S(1)} %get-tuple-element.6.a, bf16[1024,512]{1,0:T(8,128)(2,1)S(1)} %get-tuple-element.7.b, f32[4,1024]{1,0:T(4,128)S(1)} %get-tuple-element.8.d), custom_call_target="tpu_custom_call" | custom-call | bytes 2097152 | tf_op jit(solution)/shard_map/pallas_call | solution.py:448

commit v4 on v3

--- a/solution.py
+++ b/solution.py
@@ -138,7 +138,7 @@
             zz = lax.rem(z + nz - j - 1, nz)
             remote(gat.at[c, x, zz], gat.at[c, x, zz], wz_s.at[j], wz_r.at[j], sibling).wait_recv()
         loop(nz - 1, arrived)
-        for j in range(nx - 1):
+        for j in (1, 0, 2):
             wx(j).start()
         wc(0).start()
 
@@ -300,7 +300,7 @@
                 else:
                     xs[ph][j - 1, zz] = total.astype(BF16)
         loop(nz, body)
-        for j in range(nx - 1):
+        for j in (1, 0, 2):
             gx(ph, j).start()
 
     def wg_along_z(ph):
@@ -358,10 +358,10 @@
     cp_code.wait()
     cp_scale.wait()
     w_first()
+    ag_hop(1)
+    w_along_x()
     cp_tok.wait()
     turn()
-    ag_hop(1)
-    w_along_x()
     for h in range(2, hops - 1):
         ag_hop(h)
     wg_theirs(0)

time: 69.3 us -> 69.2 us (level)
  no operation moved by 1% of the time
where the time goes in v4:
time: 69.2 us; the launch traced here: 68.2 us
  Pallas kernels  67.5 us (98%)
    pallas_call x1, Pallas kernels, on_device(): pl.pallas_call(functools.partial(kernel, ny, nz, nx), out_shape=tuple((v(...  66.4 us

profile of v4, /device:TPU:1, one launch (start us, length us, event | category | flops | bytes accessed | tf_op | source)
XLA Modules:
  0.0 68.2 jit_solution(5785636965226152470)
XLA Ops:
  0.6 66.4 %shard_map.67 = (bf16[1024,128]{1,0:T(8,128)(2,1)S(1)}, bf16[1024,512]{1,0:T(8,128)(2,1)S(1)}, f32[4,1024]{1,0:T(4,128)S(1)}) custom-call(bf16[1024,512]{1,0:T(8,128)(2,1)} %tok_ref.1, bf16[4,1024]{1,0:T(4,128)(2,1)} %code_ref.1, bf16[4,4]{1,0:T(4,128)(2,1)} %scale_ref.1, bf16[1024,128]{1,0:T(8,128)(2,1)} %cot_ref.1), custom_call_target="tpu_custom_call" | custom-call | flops 3221225472 | bytes 2097152 | tf_op jit(solution)/shard_map/pallas_call | solution.py:438
  67.1 1.1 %shard_map.68 = (bf16[1024,128]{1,0:T(8,128)(2,1)}, bf16[1024,512]{1,0:T(8,128)(2,1)}, f32[4,1024]{1,0:T(4,128)}) custom-call(bf16[1024,128]{1,0:T(8,128)(2,1)S(1)} %get-tuple-element.6.a, bf16[1024,512]{1,0:T(8,128)(2,1)S(1)} %get-tuple-element.7.b, f32[4,1024]{1,0:T(4,128)S(1)} %get-tuple-element.8.d), custom_call_target="tpu_custom_call" | custom-call | bytes 2097152 | tf_op jit(solution)/shard_map/pallas_call | solution.py:448
